TPU v7x, 256 devices: a whole 4x4x8 slice. The times are simulated.
256 devices in a mesh: pos: 16 (over y, z_lo, core), mom: 16 (over x, z_hi).
Axes of the slice: x: 4, y: 4, z: 8 (z_hi: 4, z_lo: 2; z = z_hi * 2 + z_lo), core: 2. Of those that a mesh axis runs over, the one named last changes fastest.
Arguments:
- quasi_probability_grid: float32 [2, 2048, 8192], P(None, 'pos', 'mom'), may hold values from 0 to 2
- potential_energy_map: float32 [2, 2048], P(None, 'pos'), may hold values from -3 to 3
- contact_inflow_states: float32 [2, 2, 8192], P(None, None, 'mom'), may hold values from 0 to 2
- crystal_kelvin_field: float32 [2048], P('pos'), may hold values from 0.6 to 1.6
- area_index_map: int32 [2048], P('pos'), may hold values from 0 to 3
- damping_ratio_per_step: float32 [4], replicated, may hold values from 0.05 to 0.5
- equilibrium_populace: float32 [4], replicated, may hold values from 0.5 to 2
- conductance_per_step: float32 [4], replicated, may hold values from 0.05 to 0.45
Outputs:
- wigner_updated: float32 [2, 2048, 8192], P(None, 'pos', 'mom')
- phonon_warmth_updated: float32 [2048], P('pos')
All inputs are finite; a program needn't handle non-finite values.
Results may differ from a plain program's by a relative error of at most 0.0003.
Values sent between devices are 32-bit elements; how exact they have to be, the bound alone decides.
No kernel may reach another device: no remote copies, remote signals or barrier semaphores. Data moves between devices by JAX's collectives and lax.ppermute only.
A program may use at most 64 MiB of HBM per device.

v0:
```python
import functools

import jax
import jax.numpy as jnp
import numpy as np
from jax import lax
from jax.experimental import pallas as pl
from jax.experimental.pallas import tpu as pltpu
from jax.sharding import PartitionSpec as P

K = 8192
LANES = 128
RESIDUES = 64
ROWS = 16
ORDER = [14, 10, 8, 7, 13, 6, 12, 2, 5, 11, 0, 1, 3, 15, 9, 4]
BACK_ORDER = [7, 2, 14, 8, 13, 11, 15, 3, 10, 5, 6, 1, 0, 9, 4, 12]
HALF = (0, 1, 4, 5, 8, 9, 12, 13)
FLAT = 65

courant = 0.9
energy_top = 3.0
energy_shift = 0.25
band_offset = 0.5
potential_gain = 0.5
heat_gain = 0.5
heat_outflow = 0.1

RESIDUE_LIST = [u1 + 8 * u0 for u1 in (1, 2, 3) for u0 in range(8)] + [4, 12, 20, 28, 0, 8, 16, 24, 32]
COUNT = len(RESIDUE_LIST)
PLACE = {u: n for n, u in enumerate(RESIDUE_LIST)}
ROOT = float(np.sqrt(0.5))


def tables():
    idx = np.arange(LANES)
    angle = 2.0 * np.pi / LANES * (idx[:, None] * idx[None, :] % LANES)
    cos, sin = np.cos(angle), np.sin(angle)
    ahead = np.block([[cos, sin], [-sin, cos]]).astype(np.float32)

    def parts(matrix):
        high = matrix.astype(jnp.bfloat16)
        low = (matrix - high.astype(np.float32)).astype(jnp.bfloat16)
        return np.stack([high, low])

    turn = 2.0 * np.pi / K * (np.array(RESIDUE_LIST)[:, None] * idx[None, :])
    twist = np.stack([np.cos(turn), np.sin(turn)], axis=1).astype(np.float32)
    return parts(ahead), parts(np.ascontiguousarray(ahead.T)), twist


def owner_number():
    mom, rank = lax.axis_index("mom"), 0
    for n, device in enumerate(ORDER):
        rank = rank + jnp.where(mom == device, n, 0)
    return rank


def add(a, b):
    return (a[0] + b[0], a[1] + b[1])


def sub(a, b):
    return (a[0] - b[0], a[1] - b[1])


def times_i(a):
    return (-a[1], a[0])


def turned(a, angle):
    c, s = float(np.cos(angle)), float(np.sin(angle))
    return (a[0] * c - a[1] * s, a[0] * s + a[1] * c)


def real_8(f):
    a0, a1, b0, b1 = f[0] + f[4], f[0] - f[4], f[2] + f[6], f[2] - f[6]
    c0, c1, d0, d1 = f[1] + f[5], f[1] - f[5], f[3] + f[7], f[3] - f[7]
    even, odd = a0 + b0, c0 + d0
    less, more = ROOT * (c1 - d1), ROOT * (c1 + d1)
    return even + odd, (a1 + less, b1 + more), (a0 - b0, c0 - d0), (a1 - less, more - b1), even - odd


def back_8(x0, d1, d2, d3, x4):
    even, odd = x0 + x4, x0 - x4
    (r1, i1), (r2, i2), (r3, i3) = d1, d2, d3
    ea, eb = even + r2, even - r2
    sr, si = r1 + r3, i3 - i1
    oa, ob = odd - i2, odd + i2
    p, q = ROOT * (r1 - i1), ROOT * (r1 + i1)
    v, w = ROOT * (r3 + i3), ROOT * (r3 - i3)
    pv, wq = p - v, w - q
    return [ea + sr, oa + pv, eb + si, ob + wq, ea - sr, oa - pv, eb - si, ob - wq]


def complex_4(x):
    a, b, c, d = add(x[0], x[2]), sub(x[0], x[2]), add(x[1], x[3]), times_i(sub(x[1], x[3]))
    return [add(a, c), add(b, d), sub(a, c), sub(b, d)]


def complex_8(x):
    e, o = complex_4(x[0::2]), complex_4(x[1::2])
    o[1] = (ROOT * (o[1][0] - o[1][1]), ROOT * (o[1][0] + o[1][1]))
    o[2] = times_i(o[2])
    o[3] = (-ROOT * (o[3][0] + o[3][1]), ROOT * (o[3][0] - o[3][1]))
    return [add(e[n], o[n]) for n in range(4)] + [sub(e[n], o[n]) for n in range(4)]


def cs(n):
    return float(np.cos(np.pi * n / 8)), float(np.sin(np.pi * n / 8))


def odd_ahead(a):
    less = [None] + [a[q] - a[8 - q] for q in (1, 2, 3)]
    more = [None] + [a[q] + a[8 - q] for q in (1, 2, 3)]
    out = [None] * 4
    for u in (0, 1):
        n = 1 + 2 * u
        even_r = a[0] + less[2] * cs(2 * n)[0]
        odd_r = less[1] * cs(n)[0] + less[3] * cs(3 * n)[0]
        even_i = more[2] * cs(2 * n)[1]
        odd_i = more[1] * cs(n)[1] + more[3] * cs(3 * n)[1]
        even_i = even_i + a[4] if u == 0 else even_i - a[4]
        out[u] = (even_r + odd_r, odd_i + even_i)
        out[3 - u] = (even_r - odd_r, odd_i - even_i)
    return out


def odd_back(c):
    (r0, i0), (r1, i1), (r2, i2), (r3, i3) = c
    rp0, rm0, rp1, rm1 = r0 + r3, r0 - r3, r1 + r2, r1 - r2
    ip0, im0, ip1, im1 = i0 + i3, i0 - i3, i1 + i2, i1 - i2
    out = [None] * 8
    out[0] = rp0 + rp1
    out[4] = (i1 + i3) - (i0 + i2)
    for q in (1, 2, 3):
        (c0, s0), (c1, s1) = cs(q), cs(3 * q)
        if q % 2:
            cosines, sines = rm0 * c0 + rm1 * c1, ip0 * s0 + ip1 * s1
        else:
            cosines, sines = rp0 * c0 + rp1 * c1, im0 * s0 + im1 * s1
        out[q], out[8 - q] = cosines - sines, -cosines - sines
    return out


def split(value):
    high = value.astype(jnp.bfloat16)
    return high, (value - high.astype(jnp.float32)).astype(jnp.bfloat16)


def product(high, low, weights):
    dot = functools.partial(jnp.dot, preferred_element_type=jnp.float32)
    return dot(high, weights[0]) + (dot(high, weights[1]) + dot(low, weights[0]))


def transform_kernel(rows_ref, weight_ref, lattice_ref, gain_ref, ahead_ref, back_ref, twist_ref, out_ref,
                     stage, high, low, result):
    splits = rows_ref.shape[0]
    per = RESIDUES // splits

    lane = lax.broadcasted_iota(jnp.int32, (1, LANES), 1).astype(jnp.float32)

    def cell(q):
        n = (q % per) * LANES
        return rows_ref[ORDER.index(q // per), :, n : n + LANES]

    total = jnp.zeros((ROWS, LANES), jnp.float32)
    for q0 in range(8):
        f = []
        for q1 in range(8):
            q = q1 * 8 + q0
            value = cell(q)
            unit = (2.0 * (lane + float(q * LANES)) + 1.0) / K - 1.0
            total = total + value * (energy_top * (unit + energy_shift) ** 2)
            f.append(value)
        x0, x1, x2, x3, x4 = real_8(f)
        for n, value in enumerate((x0, x1[0], x1[1], x2[0], x2[1], x3[0], x3[1], x4)):
            stage[q0 * 8 + n] = value
    lattice = lattice_ref[...] + gain_ref[...] * jnp.sum(total, axis=1, keepdims=True)

    def send(u, value):
        n = PLACE[u]
        real, imag = value
        c, s = twist_ref[n, 0:1, :], twist_ref[n, 1:2, :]
        if imag is None:
            real, imag = real * c, real * s
        else:
            real, imag = real * c - imag * s, real * s + imag * c
        for half, part in ((0, real), (1, imag)):
            h, l = split(part)
            place = (slice(n * ROWS, n * ROWS + ROWS), slice(half * LANES, half * LANES + LANES))
            high[place] = h
            low[place] = l

    for u1 in (1, 2, 3):
        x = [(stage[q0 * 8 + 2 * u1 - 1], stage[q0 * 8 + 2 * u1]) for q0 in range(8)]
        x = [x[0]] + [turned(x[q0], 2.0 * np.pi * q0 * u1 / 64) for q0 in range(1, 8)]
        for u0, value in enumerate(complex_8(x)):
            send(u1 + 8 * u0, value)
    for u0, value in enumerate(odd_ahead([stage[q0 * 8 + 7] for q0 in range(8)])):
        send(4 + 8 * u0, value)
    x0, x1, x2, x3, x4 = real_8([stage[q0 * 8] for q0 in range(8)])
    for u, value in ((0, (x0, None)), (8, x1), (16, x2), (24, x3), (32, (x4, None))):
        send(u, value)

    for n in range(0, COUNT, 11):
        rows = slice(n * ROWS, (n + 11) * ROWS)
        spectrum = product(high[rows], low[rows], ahead_ref)
        weight = weight_ref[rows]
        h0, l0 = split(spectrum[:, :LANES] * weight)
        h1, l1 = split(spectrum[:, LANES:] * weight)
        result[rows] = product(
            jnp.concatenate([h0, h1], axis=1), jnp.concatenate([l0, l1], axis=1), back_ref
        )

    def fetch(u):
        n = PLACE[u]
        rows = slice(n * ROWS, n * ROWS + ROWS)
        real, imag = result[rows, :LANES], result[rows, LANES:]
        c, s = twist_ref[n, 0:1, :], twist_ref[n, 1:2, :]
        return imag * c - real * s, real * c + imag * s

    for u1 in (1, 2, 3):
        d = complex_8([fetch(u1 + 8 * u0) for u0 in range(8)])
        for q0 in range(8):
            value = turned(d[q0], 2.0 * np.pi * q0 * u1 / 64) if q0 else d[0]
            stage[q0 * 8 + 2 * u1 - 1] = value[0]
            stage[q0 * 8 + 2 * u1] = value[1]
    for q0, value in enumerate(odd_back([fetch(4 + 8 * u0) for u0 in range(4)])):
        stage[q0 * 8 + 7] = value
    ends = back_8(fetch(0)[0], fetch(8), fetch(16), fetch(24), fetch(32)[0])
    for q0, value in enumerate(ends):
        stage[q0 * 8] = value
    for q0 in range(8):
        d = [stage[q0 * 8 + n] for n in range(8)]
        for q1, value in enumerate(back_8(d[0], (d[1], d[2]), (d[3], d[4]), (d[5], d[6]), d[7])):
            q = q1 * 8 + q0
            m, jb = BACK_ORDER.index(q // per), q % per
            first = m * FLAT + jb * ROWS
            out_ref[first : first + ROWS, :] = value
    base = (owner_number() % (splits // 2)) * ROWS
    lane = lax.broadcasted_iota(jnp.int32, (ROWS, LANES), 1)
    place = lane == lax.broadcasted_iota(jnp.int32, (ROWS, LANES), 0) + base
    heat = jnp.sum(jnp.where(place, lattice, 0.0), axis=0, keepdims=True)
    for m in range(splits):
        out_ref[m * FLAT + RESIDUES : m * FLAT + FLAT, :] = heat


def pack_kernel(first_ref, last_ref, line_ref, after_ref, near_ref, far_ref):
    del after_ref
    even = lax.axis_index("pos") % 2 == 0
    for b in range(2):
        first, last = first_ref[b, 0:1, :], last_ref[b, 7:8, :]
        near, far = jnp.where(even, last, first), jnp.where(even, first, last)
        for n in range(4):
            place, lanes = slice(b * 4 + n, b * 4 + n + 1), slice(n * LANES, n * LANES + LANES)
            near_ref[place, :] = near[:, lanes]
            far_ref[place, :] = far[:, lanes]
    for out_ref in (near_ref, far_ref):
        out_ref[8:9, :] = line_ref[...]
        out_ref[9:16, :] = jnp.zeros((7, LANES), jnp.float32)


def column(row, count, first=0):
    lane = lax.broadcasted_iota(jnp.int32, (count, LANES), 1)
    place = lane == lax.broadcasted_iota(jnp.int32, (count, LANES), 0) + first
    return jnp.sum(jnp.where(place, row, 0.0), axis=1, keepdims=True)


def energy_kernel(line_ref, area_ref, damping_ref, populace_ref, after_ref, lattice_ref, gain_ref):
    del after_ref
    owner = owner_number()
    per_band = lax.axis_size("mom") // 2
    band = (owner // per_band).astype(jnp.float32)
    base = (owner % per_band) * ROWS
    inverse = column(-1.0 / line_ref[...], ROWS, base)
    gain = heat_gain / K * column(chosen(area_ref[...], damping_ref), ROWS, base)
    dens = column(chosen(area_ref[...], populace_ref), ROWS, base)
    lane = lax.broadcasted_iota(jnp.int32, (1, LANES), 1).astype(jnp.float32)
    total = jnp.zeros((ROWS, LANES), jnp.float32)
    for q in range(RESIDUES):
        unit = (2.0 * (lane + float(q * LANES)) + 1.0) / K - 1.0
        energy = energy_top * (unit + energy_shift) ** 2
        total = total + energy * jnp.exp((energy + band_offset * band) * inverse)
    lattice_ref[...] = -gain * dens * jnp.sum(total, axis=1, keepdims=True)
    gain_ref[...] = gain


def chosen(area, table_ref):
    value = jnp.zeros(area.shape, jnp.float32)
    for n in range(table_ref.shape[0]):
        value = value + jnp.where(area == n, table_ref[n], 0.0)
    return value


def potential_kernel(half_ref, other_ref, weight_ref, profile, ahead_t, behind_t, ahead_w, behind_w):
    spot, owner = lax.axis_index("pos"), owner_number()
    spots = profile.shape[0]
    per_band = lax.axis_size("mom") // 2
    partner = (spot + jnp.where(spot % 2 == 0, spots - 1, 1)) % spots
    for home, ref in ((spot, half_ref), (partner, other_ref)):
        for n, offset in enumerate(HALF):
            row = jnp.where(owner < per_band, ref[2 * n : 2 * n + 1, :], ref[2 * n + 1 : 2 * n + 2, :])
            profile[pl.ds(home ^ offset, 1), :] = row
    first, last = profile[0:1, 0:1], profile[spots - 1 : spots, LANES - 1 : LANES]
    start = spot * LANES + (owner % per_band) * ROWS
    lead = start // RESIDUES
    inner = pl.multiple_of(start % RESIDUES, 8)
    source = lax.broadcasted_iota(jnp.int32, (spots, LANES), 0)
    lane = lax.broadcasted_iota(jnp.int32, (spots, LANES), 1)
    mirror = (LANES - lane) % LANES
    window = ahead_w.shape[0]
    row_w = lax.broadcasted_iota(jnp.int32, (window, LANES), 0)
    lane_w = lax.broadcasted_iota(jnp.int32, (window, LANES), 1)
    carry = (inner + row_w) // RESIDUES - 1
    ahead_q = lead + carry + lane_w - jnp.where(lane_w >= RESIDUES, LANES, 0)
    behind_q = lead + carry - lane_w + jnp.where(lane_w >= RESIDUES, LANES, 0)
    cells = spots * LANES // RESIDUES

    def pick(place):
        pieces = []
        for h in range(2):
            chooser = jnp.where(place == 2 * source + h, 1.0, 0.0)
            full = lax.dot_general(
                profile[...], chooser, (((0,), (0,)), ((), ())),
                precision=lax.Precision.HIGHEST, preferred_element_type=jnp.float32,
            )
            pieces.append(full[h * RESIDUES : h * RESIDUES + RESIDUES])
        return pieces[0] + pieces[1]

    forward, backward = pick(lane), pick(mirror)
    for n, k in enumerate((-1, 0, 1)):
        rows = slice(n * RESIDUES, n * RESIDUES + RESIDUES)
        ahead_t[rows] = pltpu.roll(forward, (-k) % LANES, 1) if k else forward
        behind_t[rows] = pltpu.roll(backward, k % LANES, 1) if k else backward
    for table, wide, shift, q in (
        (ahead_t, ahead_w, (LANES - lead) % LANES, ahead_q),
        (behind_t, behind_w, lead, behind_q),
    ):
        value = pltpu.roll(table[pl.ds(inner, window), :], shift, 1)
        value = jnp.where(q < 0, first, value)
        wide[...] = jnp.where(q >= cells, last, value)
    for n, u in enumerate(RESIDUE_LIST):
        scale = potential_gain / K * (1.0 if u in (0, 32) else 2.0)
        ahead = ahead_w[RESIDUES + u : RESIDUES + u + ROWS, :]
        behind = behind_w[RESIDUES - u : RESIDUES - u + ROWS, :]
        weight_ref[n * ROWS : n * ROWS + ROWS, :] = scale * (ahead - behind)


def local_kernel(grid_ref, near_ref, far_ref, contact_ref, line_ref, area_ref, damping_ref, populace_ref,
                 conductance_ref, after_ref, out_ref, still_ref):
    del after_ref
    spot, mom = lax.axis_index("pos"), lax.axis_index("mom")
    spots = lax.axis_size("pos")
    even = spot % 2 == 0
    _, rows, count = grid_ref.shape
    place = lax.broadcasted_iota(jnp.int32, (1, LANES), 1)
    row = lax.broadcasted_iota(jnp.int32, (rows, LANES), 0)
    kelvin, area = line_ref[...], area_ref[...]
    inverse = column(-1.0 / kelvin, rows)
    relax = column(chosen(area, damping_ref), rows)
    dens = column(chosen(area, populace_ref), rows)
    for n in range(count // LANES):
        lanes = slice(n * LANES, n * LANES + LANES)
        unit = (2.0 * (place + (mom * count + n * LANES)).astype(jnp.float32) + 1.0) / K - 1.0
        velocity = courant * unit
        energy = energy_top * (unit + energy_shift) ** 2
        for b in range(2):
            f = grid_ref[b, :, lanes]
            edge = b * 4 + n
            near, far = near_ref[edge : edge + 1, :], far_ref[16 + edge : 17 + edge, :]
            before = jnp.where(spot == 0, contact_ref[b, 0:1, lanes], jnp.where(even, far, near))
            after = jnp.where(spot == spots - 1, contact_ref[b, 1:2, lanes], jnp.where(even, near, far))
            below = jnp.where(row == 0, before, pltpu.roll(f, 1, 0))
            above = jnp.where(row == rows - 1, after, pltpu.roll(f, rows - 1, 0))
            drift = velocity * jnp.where(velocity > 0, below - f, f - above)
            excess = f - dens * jnp.exp((energy + band_offset * b) * inverse)
            out_ref[b, :, lanes] = f + drift - relax * excess

    near, far = near_ref[8:9, :], far_ref[24:25, :]
    below = jnp.where(spot == 0, 1.0, jnp.where(even, far, near)[:, LANES - 1 : LANES])
    above = jnp.where(spot == spots - 1, 1.0, jnp.where(even, near, far)[:, 0:1])
    lower = jnp.where(place == 0, below, pltpu.roll(kelvin, 1, 1))
    upper = jnp.where(place == LANES - 1, above, pltpu.roll(kelvin, LANES - 1, 1))
    flow = chosen(area, conductance_ref) * (upper - 2.0 * kelvin + lower)
    still_ref[...] = kelvin + flow - heat_outflow * (kelvin - 1.0)


def final_kernel(base_ref, back_ref, still_ref, out_ref, lattice_ref):
    splits = back_ref.shape[0] // FLAT
    per_band = splits // 2
    lattice = still_ref[...]
    for m in range(splits):
        owner = ORDER.index(BACK_ORDER[m])
        b, first = owner // per_band, (owner % per_band) * ROWS
        rows = slice(first, first + ROWS)
        for n in range(4):
            lanes = slice(n * LANES, n * LANES + LANES)
            start = m * FLAT + n * ROWS
            out_ref[b, rows, lanes] = base_ref[b, rows, lanes] + back_ref[start : start + ROWS, :]
        lattice = lattice + back_ref[m * FLAT + RESIDUES : m * FLAT + FLAT, :]
    lattice_ref[...] = lattice


VM = pl.BlockSpec(memory_space=pltpu.VMEM)
SM = pl.BlockSpec(memory_space=pltpu.SMEM)


def call(kernel, outs, specs, flops=0, moved=0, scratch=(), **more):
    return pl.pallas_call(
        kernel,
        out_shape=outs,
        in_specs=specs,
        out_specs=jax.tree.map(lambda _: VM, outs),
        scratch_shapes=list(scratch),
        compiler_params=pltpu.CompilerParams(vmem_limit_bytes=32 * 2**20),
        cost_estimate=pl.CostEstimate(flops=flops, bytes_accessed=moved, transcendentals=0),
        **more,
    )


def f32(*shape):
    return jax.ShapeDtypeStruct(shape, jnp.float32)


def body(grid, potential, contact, kelvin, area, damping, populace, conductance):
    bands, rows, count = grid.shape
    spots, splits = lax.axis_size("pos"), lax.axis_size("mom")
    ahead, back, twist = tables()

    def swapped(value, mask):
        return lax.ppermute(value, "pos", [(n ^ mask, n) for n in range(spots)])

    def exchanged(value, order):
        return lax.all_to_all(value, "mom", split_axis=0, concat_axis=0, axis_index_groups=[order])

    full = exchanged(grid.reshape(splits, ROWS, count), ORDER)
    kelvin_row, area_row = kelvin.reshape(1, rows), area.reshape(1, rows)
    pair = jnp.concatenate([potential, swapped(potential, 1)], axis=0)
    message = pl.BlockSpec((16, LANES), lambda i: (0, 0))
    core, outer = pl.pallas_call(
        pack_kernel,
        grid=(1,),
        out_shape=(f32(16, LANES), f32(16, LANES)),
        in_specs=[
            pl.BlockSpec((bands, 8, count), lambda i: (0, 0, 0)),
            pl.BlockSpec((bands, 8, count), lambda i: (0, rows // 8 - 1, 0)),
            pl.BlockSpec((1, rows), lambda i: (0, 0)),
            pl.BlockSpec(memory_space=pl.ANY),
        ],
        out_specs=(message, message),
        cost_estimate=pl.CostEstimate(flops=1000, bytes_accessed=1000, transcendentals=0),
    )(grid, grid, kelvin_row, pair)
    outer = jnp.concatenate([pair, swapped(pair, 4), swapped(pair, 8), swapped(pair, 12), outer], axis=0)
    far = lax.ppermute(outer, "pos", [((n + (1 if n % 2 else -1)) % spots, n) for n in range(spots)])

    near = swapped(core, 1)

    weight = call(
        potential_kernel,
        f32(COUNT * ROWS, LANES),
        [VM] * 2,
        flops=1000,
        moved=1000,
        scratch=[
            pltpu.VMEM((spots, LANES), jnp.float32),
            pltpu.VMEM((3 * RESIDUES, LANES), jnp.float32),
            pltpu.VMEM((3 * RESIDUES, LANES), jnp.float32),
            pltpu.VMEM((144, LANES), jnp.float32),
            pltpu.VMEM((144, LANES), jnp.float32),
        ],
    )(outer, far)
    lattice, gain = call(
        energy_kernel,
        (f32(ROWS, 1), f32(ROWS, 1)),
        [VM] * 2 + [SM] * 2 + [pl.BlockSpec(memory_space=pl.ANY)],
        flops=1000,
        moved=1000,
    )(kelvin_row, area_row, damping, populace, outer)
    messages = call(
        transform_kernel,
        f32(splits * FLAT, LANES),
        [VM] * 7,
        flops=10**9,
        moved=2**21,
        scratch=[
            pltpu.VMEM((RESIDUES, ROWS, LANES), jnp.float32),
            pltpu.VMEM((COUNT * ROWS, 2 * LANES), jnp.bfloat16),
            pltpu.VMEM((COUNT * ROWS, 2 * LANES), jnp.bfloat16),
            pltpu.VMEM((COUNT * ROWS, 2 * LANES), jnp.float32),
        ],
    )(full, weight, lattice, gain, jnp.asarray(ahead), jnp.asarray(back), jnp.asarray(twist))
    received = exchanged(messages.reshape(splits, FLAT, 1, LANES), BACK_ORDER).reshape(splits * FLAT, LANES)

    base, still = call(
        local_kernel,
        (f32(bands, rows, count), f32(1, rows)),
        [VM] * 6 + [SM] * 3 + [pl.BlockSpec(memory_space=pl.ANY)],
        flops=1000,
        moved=1000,
    )(grid, near, far, contact, kelvin_row, area_row, damping, populace, conductance, messages)
    updated, warmth = call(
        final_kernel, (f32(bands, rows, count), f32(1, rows)), [VM] * 3, flops=10**6, moved=2**21
    )(base, received, still)
    return updated, warmth.reshape(rows)


def solution(mesh):
    return jax.shard_map(
        body,
        mesh=mesh,
        in_specs=(
            P(None, "pos", "mom"),
            P(None, "pos"),
            P(None, None, "mom"),
            P("pos"),
            P("pos"),
            P(),
            P(),
            P(),
        ),
        out_specs=(P(None, "pos", "mom"), P("pos")),
        check_vma=False,
    )
```

profile of v0, /device:TPU:32, one launch (start us, length us, event | category | flops | bytes accessed | tf_op | source)
XLA Modules:
  0.0 51.0 jit_solution(15675562762815438941)
XLA Ops:
  0.6 0.0 copy-start.11
  0.6 12.1 %all-to-all-start = ((f32[16,16,512]{2,1,0:T(8,128)}), f32[16,16,512]{2,1,0:T(8,128)S(1)}, u32[]{:S(2)}, u32[]{:S(2)}) async-start(f32[16,16,512]{2,1,0:T(8,128)} %bitcast.6), calls=%async_computation | async-start | bytes 1048576 | tf_op jit(solution)/shard_map/all_to_all | solution.py:433
  12.7 0.0 copy-done.11
  12.7 0.1 collective-permute-start
  12.8 1.1 %collective-permute-done = f32[2,128]{1,0:T(2,128)S(1)} collective-permute-done((f32[2,128]{1,0:T(2,128)S(1)}, f32[2,128]{1,0:T(2,128)S(1)}, u32[]{:S(2)}, u32[]{:S(2)}) %collective-permute-start) | collective-permute-done | bytes 1056 | tf_op jit(solution)/shard_map/ppermute | solution.py:430
  14.0 0.0 copy-start.10
  14.0 1.7 %collective-permute-start.2 = (f32[4,128]{1,0:T(4,128)S(1)}, f32[4,128]{1,0:T(4,128)S(1)}, u32[]{:S(2)}, u32[]{:S(2)}) collective-permute-start(f32[4,128]{1,0:T(4,128)S(1)} %pad_maximum_fusion.after_ref), channel_id=1, source_target_pairs={{64,0},{80,16},{96,32},{112,48},{0,64},{16,80},{32,96},{48,112},{1... | collective-permute-start | bytes 6152 | tf_op jit(solution)/shard_map/ppermute | solution.py:430
  15.7 2.9 %collective-permute-start.3 = (f32[4,128]{1,0:T(4,128)S(1)}, f32[4,128]{1,0:T(4,128)S(1)}, u32[]{:S(2)}, u32[]{:S(2)}) collective-permute-start(f32[4,128]{1,0:T(4,128)S(1)} %pad_maximum_fusion.after_ref), channel_id=1, source_target_pairs={{128,0},{144,16},{160,32},{176,48},{192,64},{208,80},{224,96},{240... | collective-permute-start | bytes 6152 | tf_op jit(solution)/shard_map/ppermute | solution.py:430
  18.6 0.2 collective-permute-start.4
  18.8 0.0 copy-done.10
  18.8 0.0 copy-start.7
  18.8 0.0 copy-start.8
  18.8 1.4 %shard_map.122 = (f32[16,128]{1,0:T(8,128)}, f32[16,128]{1,0:T(8,128)}) custom-call(f32[2,128,512]{2,1,0:T(8,128)} %grid_ref.1, f32[2,128,512]{2,1,0:T(8,128)} %grid_ref.1, f32[1,128]{1,0:T(1,128)} %bitcast.8, f32[4,128]{1,0:T(4,128)} %copy-done.10), custom_call_target="tpu_custom_call" | custom-call | flops 1000 | bytes 1000 | tf_op jit(solution)/shard_map/pallas_call | solution.py:439
  20.2 0.0 collective-permute-done.2
  20.2 0.5 %collective-permute-done.3 = f32[4,128]{1,0:T(4,128)S(1)} collective-permute-done((f32[4,128]{1,0:T(4,128)S(1)}, f32[4,128]{1,0:T(4,128)S(1)}, u32[]{:S(2)}, u32[]{:S(2)}) %collective-permute-start.3) | collective-permute-done | bytes 2080 | tf_op jit(solution)/shard_map/ppermute | solution.py:430
  20.7 2.6 %collective-permute-done.4 = f32[4,128]{1,0:T(4,128)S(1)} collective-permute-done((f32[4,128]{1,0:T(4,128)S(1)}, f32[4,128]{1,0:T(4,128)S(1)}, u32[]{:S(2)}, u32[]{:S(2)}) %collective-permute-start.4) | collective-permute-done | bytes 2080 | tf_op jit(solution)/shard_map/ppermute | solution.py:430
  23.4 0.0 copy-start.5
  23.4 0.7 %concatenate.8.half_ref.after_ref = f32[32,128]{1,0:T(8,128)S(1)} concatenate(f32[2,128]{1,0:T(2,128)S(1)} %copy-done.11, f32[2,128]{1,0:T(2,128)S(1)} %collective-permute-done, f32[4,128]{1,0:T(4,128)S(1)} %collective-permute-done.2, f32[4,128]{1,0:T(4,128)S(1)} %collective-permute-done.3, f32[4,128]{1,0:T(4,128)S(1)} %collective-permute-done.4, f32[16,128]{1,0:T(8,128)} %get-tuple-element.11), dimensions={0} | concatenate | bytes 32768 | tf_op jit(solution)/shard_map/concatenate | solution.py:452
  24.1 0.0 copy-start.2
  24.1 0.0 copy-start.3
  24.1 0.0 copy-start.4
  24.1 0.0 collective-permute-start.5
  24.1 0.0 copy-done.5
  24.1 0.6 %copy-done.2 = f32[128]{0:T(128)S(1)} copy-done((f32[128]{0:T(128)S(1)}, f32[128]{0:T(128)}, u32[]{:S(2)}) %copy-start.2) | copy-done | bytes 536
  24.7 0.0 copy-done.3
  24.8 0.0 copy-done.4
  24.8 0.8 %shard_map.124 = (f32[16,1]{1,0:T(8,128)S(1)}, f32[16,1]{1,0:T(8,128)S(1)}) custom-call(f32[1,128]{1,0:T(1,128)S(1)} %bitcast.9, s32[1,128]{1,0:T(1,128)S(1)} %bitcast.11, f32[4]{0:T(128)S(1)} %copy-done.4, f32[4]{0:T(128)S(1)} %copy-done.5, f32[32,128]{1,0:T(8,128)S(1)} %concatenate.8.half_ref.after_ref), custom_call_target="tpu_custom_call" | custom-call | flops 1000 | bytes 1000 | tf_op jit(solution)/shard_map/pallas_call | solution.py:471
  25.6 0.0 copy-start.9
  25.6 1.6 %collective-permute-done.5.other_ref.far_ref = f32[32,128]{1,0:T(8,128)S(1)} collective-permute-done((f32[32,128]{1,0:T(8,128)S(1)}, f32[32,128]{1,0:T(8,128)S(1)}, u32[]{:S(2)}, u32[]{:S(2)}) %collective-permute-start.5) | collective-permute-done | bytes 16416 | tf_op jit(solution)/shard_map/ppermute | solution.py:453
  27.3 0.7 %shard_map.123.weight_ref = f32[528,128]{1,0:T(8,128)S(1)} custom-call(f32[32,128]{1,0:T(8,128)S(1)} %concatenate.8.half_ref.after_ref, f32[32,128]{1,0:T(8,128)S(1)} %collective-permute-done.5.other_ref.far_ref), custom_call_target="tpu_custom_call" | custom-call | flops 1000 | bytes 1000 | tf_op jit(solution)/shard_map/pallas_call | solution.py:457
  28.0 0.0 all-to-all-done.rows_ref
  28.0 0.0 copy-done.7
  28.0 0.0 copy-done.8
  28.0 0.0 copy-done.9
  28.0 1.8 %shard_map.125.after_ref = f32[1040,128]{1,0:T(8,128)} custom-call(f32[16,16,512]{2,1,0:T(8,128)S(1)} %all-to-all-done.rows_ref, f32[528,128]{1,0:T(8,128)S(1)} %shard_map.123.weight_ref, f32[16,1]{1,0:T(8,128)S(1)} %get-tuple-element.12.lattice_ref, f32[16,1]{1,0:T(8,128)S(1)} %get-tuple-element.13.gain_ref, bf16[2,256,256]{2,1,0:T(8,128)(2,1)S(1)} %copy-done.7, ...), custom_call_target="tpu_custom_call" | custom-call | flops 1000000000 | bytes 2097152 | tf_op jit(solution)/shard_map/pallas_call | solution.py:478
  29.9 0.0 copy-start.12
  29.9 0.0 copy-start
  29.9 0.0 copy-start.1
  29.9 6.5 %all-to-all-start.1 = ((f32[16,65,1,128]{3,2,1,0:T(1,128)}), f32[16,65,1,128]{3,2,1,0:T(1,128)S(1)}, u32[]{:S(2)}, u32[]{:S(2)}) async-start(f32[16,65,1,128]{3,2,1,0:T(1,128)} %bitcast.3), calls=%async_computation.1 | async-start | bytes 1064960 | tf_op jit(solution)/shard_map/all_to_all | solution.py:433
  36.3 0.0 copy-start.6
  36.3 0.0 copy-done.12
  36.3 0.1 collective-permute-start.1
  36.4 1.2 %collective-permute-done.1.near_ref = f32[16,128]{1,0:T(8,128)S(1)} collective-permute-done((f32[16,128]{1,0:T(8,128)S(1)}, f32[16,128]{1,0:T(8,128)S(1)}, u32[]{:S(2)}, u32[]{:S(2)}) %collective-permute-start.1) | collective-permute-done | bytes 8224 | tf_op jit(solution)/shard_map/ppermute | solution.py:430
  37.6 0.0 copy-done
  37.6 0.0 copy-done.1
  37.6 0.0 copy-done.6
  37.6 1.0 %shard_map.126 = (f32[2,128,512]{2,1,0:T(8,128)S(1)}, f32[1,128]{1,0:T(1,128)S(1)}) custom-call(f32[2,128,512]{2,1,0:T(8,128)S(1)} %copy-done, f32[16,128]{1,0:T(8,128)S(1)} %collective-permute-done.1.near_ref, f32[32,128]{1,0:T(8,128)S(1)} %collective-permute-done.5.other_ref.far_ref, f32[2,2,512]{2,1,0:T(2,128)S(1)} %copy-done.1, f32[1,128]{1,0:T(1,128)S(1)} %bitcast.10, ...), custom_call_target="tpu_custom_call" | custom-call | flops 1000 | bytes 1000 | tf_op jit(solution)/shard_map/pallas_call | solution.py:493
  38.6 11.5 %all-to-all-done.1 = f32[16,65,1,128]{3,2,1,0:T(1,128)S(1)} async-done(((f32[16,65,1,128]{3,2,1,0:T(1,128)}), f32[16,65,1,128]{3,2,1,0:T(1,128)S(1)}, u32[]{:S(2)}, u32[]{:S(2)}) %all-to-all-start.1) | async-done | bytes 532512 | tf_op jit(solution)/shard_map/all_to_all | solution.py:433
  50.1 0.9 %shard_map.127 = (f32[2,128,512]{2,1,0:T(8,128)}, f32[1,128]{1,0:T(1,128)}) custom-call(f32[2,128,512]{2,1,0:T(8,128)S(1)} %get-tuple-element.14.base_ref, f32[1040,128]{1,0:T(8,128)S(1)} %bitcast.7, f32[1,128]{1,0:T(1,128)S(1)} %get-tuple-element.15.still_ref), custom_call_target="tpu_custom_call" | custom-call | flops 1000000 | bytes 2097152 | tf_op jit(solution)/shard_map/pallas_call | solution.py:500
  (1 shorter events, 0.0 us)
Async XLA Ops:
  0.6 12.1 %copy-start.11 = (f32[2,128]{1,0:T(2,128)S(1)}, f32[2,128]{1,0:T(2,128)}, u32[]{:S(2)}) copy-start(f32[2,128]{1,0:T(2,128)} %param.12) | copy-start | bytes 3076
  0.6 27.3 %all-to-all-start = ((f32[16,16,512]{2,1,0:T(8,128)}), f32[16,16,512]{2,1,0:T(8,128)S(1)}, u32[]{:S(2)}, u32[]{:S(2)}) async-start(f32[16,16,512]{2,1,0:T(8,128)} %bitcast.6), calls=%async_computation | async-start | bytes 1048576 | tf_op jit(solution)/shard_map/all_to_all | solution.py:433
  12.7 1.2 %collective-permute-start = (f32[2,128]{1,0:T(2,128)S(1)}, f32[2,128]{1,0:T(2,128)S(1)}, u32[]{:S(2)}, u32[]{:S(2)}) collective-permute-start(f32[2,128]{1,0:T(2,128)S(1)} %copy-done.11), channel_id=1, source_target_pairs={{16,0},{0,16},{48,32},{32,48},{80,64},{64,80},{112,96},{96,112},{1... | collective-permute-start | bytes 3080 | tf_op jit(solution)/shard_map/ppermute | solution.py:430
  14.0 4.8 %copy-start.10 = (f32[4,128]{1,0:T(4,128)}, f32[4,128]{1,0:T(4,128)S(1)}, u32[]{:S(2)}) copy-start(f32[4,128]{1,0:T(4,128)S(1)} %pad_maximum_fusion.after_ref) | copy-start | bytes 6148
  14.0 6.2 %collective-permute-start.2 = (f32[4,128]{1,0:T(4,128)S(1)}, f32[4,128]{1,0:T(4,128)S(1)}, u32[]{:S(2)}, u32[]{:S(2)}) collective-permute-start(f32[4,128]{1,0:T(4,128)S(1)} %pad_maximum_fusion.after_ref), channel_id=1, source_target_pairs={{64,0},{80,16},{96,32},{112,48},{0,64},{16,80},{32,96},{48,112},{1... | collective-permute-start | bytes 6152 | tf_op jit(solution)/shard_map/ppermute | solution.py:430
  15.7 5.1 %collective-permute-start.3 = (f32[4,128]{1,0:T(4,128)S(1)}, f32[4,128]{1,0:T(4,128)S(1)}, u32[]{:S(2)}, u32[]{:S(2)}) collective-permute-start(f32[4,128]{1,0:T(4,128)S(1)} %pad_maximum_fusion.after_ref), channel_id=1, source_target_pairs={{128,0},{144,16},{160,32},{176,48},{192,64},{208,80},{224,96},{240... | collective-permute-start | bytes 6152 | tf_op jit(solution)/shard_map/ppermute | solution.py:430
  18.6 4.8 %collective-permute-start.4 = (f32[4,128]{1,0:T(4,128)S(1)}, f32[4,128]{1,0:T(4,128)S(1)}, u32[]{:S(2)}, u32[]{:S(2)}) collective-permute-start(f32[4,128]{1,0:T(4,128)S(1)} %pad_maximum_fusion.after_ref), channel_id=1, source_target_pairs={{192,0},{208,16},{224,32},{240,48},{128,64},{144,80},{160,96},{176... | collective-permute-start | bytes 6152 | tf_op jit(solution)/shard_map/ppermute | solution.py:430
  18.8 9.2 %copy-start.7 = (bf16[2,256,256]{2,1,0:T(8,128)(2,1)S(1)}, bf16[2,256,256]{2,1,0:T(8,128)(2,1)}, u32[]{:S(2)}) copy-start(bf16[2,256,256]{2,1,0:T(8,128)(2,1)} %constant.6.clone.ahead_ref) | copy-start | bytes 786436
  18.8 9.2 %copy-start.8 = (bf16[2,256,256]{2,1,0:T(8,128)(2,1)S(1)}, bf16[2,256,256]{2,1,0:T(8,128)(2,1)}, u32[]{:S(2)}) copy-start(bf16[2,256,256]{2,1,0:T(8,128)(2,1)} %constant.7.clone.back_ref) | copy-start | bytes 786436
  23.4 0.8 %copy-start.5 = (f32[4]{0:T(128)S(1)}, f32[4]{0:T(128)}, u32[]{:S(2)}) copy-start(f32[4]{0:T(128)} %populace_ref.3) | copy-start | bytes 52
  24.1 0.7 %copy-start.2 = (f32[128]{0:T(128)S(1)}, f32[128]{0:T(128)}, u32[]{:S(2)}) copy-start(f32[128]{0:T(128)} %param.14) | copy-start | bytes 1540
  24.1 0.7 %copy-start.3 = (s32[128]{0:T(128)S(1)}, s32[128]{0:T(128)}, u32[]{:S(2)}) copy-start(s32[128]{0:T(128)} %param.15) | copy-start | bytes 1540
  24.1 0.7 %copy-start.4 = (f32[4]{0:T(128)S(1)}, f32[4]{0:T(128)}, u32[]{:S(2)}) copy-start(f32[4]{0:T(128)} %damping_ref.3) | copy-start | bytes 52
  24.1 3.2 %collective-permute-start.5 = (f32[32,128]{1,0:T(8,128)S(1)}, f32[32,128]{1,0:T(8,128)S(1)}, u32[]{:S(2)}, u32[]{:S(2)}) collective-permute-start(f32[32,128]{1,0:T(8,128)S(1)} %concatenate.8.half_ref.after_ref), channel_id=1, source_target_pairs={{240,0},{32,16},{16,32},{64,48},{48,64},{96,80},{80,96},{128,112},... | collective-permute-start | bytes 49160 | tf_op jit(solution)/shard_map/ppermute | solution.py:453
  25.6 2.4 %copy-start.9 = (f32[33,2,128]{2,1,0:T(2,128)S(1)}, f32[33,2,128]{2,1,0:T(2,128)}, u32[]{:S(2)}) copy-start(f32[33,2,128]{2,1,0:T(2,128)} %constant.8.clone.twist_ref) | copy-start | bytes 101380
  29.9 6.5 %copy-start.12 = (f32[16,128]{1,0:T(8,128)S(1)}, f32[16,128]{1,0:T(8,128)}, u32[]{:S(2)}) copy-start(f32[16,128]{1,0:T(8,128)} %get-tuple-element.10) | copy-start | bytes 24580
  29.9 7.7 %copy-start = (f32[2,128,512]{2,1,0:T(8,128)S(1)}, f32[2,128,512]{2,1,0:T(8,128)}, u32[]{:S(2)}) copy-start(f32[2,128,512]{2,1,0:T(8,128)} %grid_ref.1) | copy-start | bytes 1572868
  29.9 7.7 %copy-start.1 = (f32[2,2,512]{2,1,0:T(2,128)S(1)}, f32[2,2,512]{2,1,0:T(2,128)}, u32[]{:S(2)}) copy-start(f32[2,2,512]{2,1,0:T(2,128)} %contact_ref.1) | copy-start | bytes 24580
  29.9 20.3 %all-to-all-start.1 = ((f32[16,65,1,128]{3,2,1,0:T(1,128)}), f32[16,65,1,128]{3,2,1,0:T(1,128)S(1)}, u32[]{:S(2)}, u32[]{:S(2)}) async-start(f32[16,65,1,128]{3,2,1,0:T(1,128)} %bitcast.3), calls=%async_computation.1 | async-start | bytes 1064960 | tf_op jit(solution)/shard_map/all_to_all | solution.py:433
  36.3 1.3 %copy-start.6 = (f32[4]{0:T(128)S(1)}, f32[4]{0:T(128)}, u32[]{:S(2)}) copy-start(f32[4]{0:T(128)} %conductance_ref.1) | copy-start | bytes 52
  36.3 1.3 %collective-permute-start.1 = (f32[16,128]{1,0:T(8,128)S(1)}, f32[16,128]{1,0:T(8,128)S(1)}, u32[]{:S(2)}, u32[]{:S(2)}) collective-permute-start(f32[16,128]{1,0:T(8,128)S(1)} %copy-done.12), channel_id=1, source_target_pairs={{16,0},{0,16},{48,32},{32,48},{80,64},{64,80},{112,96},{96,112},{1... | collective-permute-start | bytes 24584 | tf_op jit(solution)/shard_map/ppermute | solution.py:430
where the time goes:
time: 51.4 us; the launch traced here: 51 us
  starting transfers between devices  23.5 us (46%)
  waiting for transfers between devices  18.5 us (36%)
  Pallas kernels  6.71 us (13%)
  local copies, waits for them, and re-layouts  1.44 us (3%)
  between operations  0.75 us (1%)
    all_to_all x2, starting transfers between devices, exchanged(): lax.all_to_all(value, 'mom', split_axis=0, concat_axis=0, axis_index_grou...  18.6 us
    all_to_all x2, waiting for transfers between devices, exchanged(): lax.all_to_all(value, 'mom', split_axis=0, concat_axis=0, axis_index_grou...  11.5 us
    ppermute x5, waiting for transfers between devices, swapped(): return lax.ppermute(value, 'pos', [(n ^ mask, n) for n in range(spots)])  5.41 us
    ppermute x5, starting transfers between devices, swapped(): return lax.ppermute(value, 'pos', [(n ^ mask, n) for n in range(spots)])  4.97 us
    pallas_call x1, Pallas kernels, body(): call(transform_kernel, f32(splits * FLAT, LANES), [VM] * 7, flops=10 ** 9...  1.85 us
    ppermute x1, waiting for transfers between devices, body(): lax.ppermute(outer, 'pos', [((n + (1 if n % 2 else -1)) % spots, n) for n...  1.63 us
    pallas_call x1, Pallas kernels, body(): pl.pallas_call(pack_kernel, grid=(1,), out_shape=(f32(16, LANES), f32(16,...  1.44 us
  transfers between devices with their start and end apart: 8, of which 6 were waited for; matrix products, arithmetic and copies ran while one was open for 1% of the time, Pallas kernels for 8%

commit v1 on v0

--- a/solution.py
+++ b/solution.py
@@ -201,8 +201,8 @@
     for u, value in ((0, (x0, None)), (8, x1), (16, x2), (24, x3), (32, (x4, None))):
         send(u, value)
 
-    for n in range(0, COUNT, 11):
-        rows = slice(n * ROWS, (n + 11) * ROWS)
+    for n in range(0, COUNT, 3):
+        rows = slice(n * ROWS, (n + 3) * ROWS)
         spectrum = product(high[rows], low[rows], ahead_ref)
         weight = weight_ref[rows]
         h0, l0 = split(spectrum[:, :LANES] * weight)

time: 51.4 us -> 52.1 us (1.014)
  Pallas kernels: 6.71 us -> 7.44 us
    pallas_call x1, Pallas kernels: 1.85 us -> 2.58 us  [body(): call(transform_kernel, f32(splits * FLAT, LANES), [VM] * 7, flops=10 ** 9...]
where the time goes in v1:
time: 52.1 us; the launch traced here: 51.7 us
  starting transfers between devices  23.5 us (45%)
  waiting for transfers between devices  18.5 us (36%)
  Pallas kernels  7.44 us (14%)
  local copies, waits for them, and re-layouts  1.44 us (3%)
  between operations  0.75 us (1%)
    all_to_all x2, starting transfers between devices, exchanged(): lax.all_to_all(value, 'mom', split_axis=0, concat_axis=0, axis_index_grou...  18.6 us
    all_to_all x2, waiting for transfers between devices, exchanged(): lax.all_to_all(value, 'mom', split_axis=0, concat_axis=0, axis_index_grou...  11.5 us
    ppermute x5, waiting for transfers between devices, swapped(): return lax.ppermute(value, 'pos', [(n ^ mask, n) for n in range(spots)])  5.41 us
    ppermute x5, starting transfers between devices, swapped(): return lax.ppermute(value, 'pos', [(n ^ mask, n) for n in range(spots)])  4.97 us
    pallas_call x1, Pallas kernels, body(): call(transform_kernel, f32(splits * FLAT, LANES), [VM] * 7, flops=10 ** 9...  2.58 us
    ppermute x1, waiting for transfers between devices, body(): lax.ppermute(outer, 'pos', [((n + (1 if n % 2 else -1)) % spots, n) for n...  1.63 us
    pallas_call x1, Pallas kernels, body(): pl.pallas_call(pack_kernel, grid=(1,), out_shape=(f32(16, LANES), f32(16,...  1.44 us
  transfers between devices with their start and end apart: 8, of which 6 were waited for; matrix products, arithmetic and copies ran while one was open for 1% of the time, Pallas kernels for 8%

profile of v1, /device:TPU:32, one launch (start us, length us, event | category | flops | bytes accessed | tf_op | source)
XLA Modules:
  0.0 51.7 jit_solution(11929189355166754377)
XLA Ops:
  0.6 0.0 copy-start.11
  0.6 12.1 %all-to-all-start = ((f32[16,16,512]{2,1,0:T(8,128)}), f32[16,16,512]{2,1,0:T(8,128)S(1)}, u32[]{:S(2)}, u32[]{:S(2)}) async-start(f32[16,16,512]{2,1,0:T(8,128)} %bitcast.6), calls=%async_computation | async-start | bytes 1048576 | tf_op jit(solution)/shard_map/all_to_all | solution.py:433
  12.7 0.0 copy-done.11
  12.7 0.1 collective-permute-start
  12.8 1.1 %collective-permute-done = f32[2,128]{1,0:T(2,128)S(1)} collective-permute-done((f32[2,128]{1,0:T(2,128)S(1)}, f32[2,128]{1,0:T(2,128)S(1)}, u32[]{:S(2)}, u32[]{:S(2)}) %collective-permute-start) | collective-permute-done | bytes 1056 | tf_op jit(solution)/shard_map/ppermute | solution.py:430
  14.0 0.0 copy-start.10
  14.0 1.7 %collective-permute-start.2 = (f32[4,128]{1,0:T(4,128)S(1)}, f32[4,128]{1,0:T(4,128)S(1)}, u32[]{:S(2)}, u32[]{:S(2)}) collective-permute-start(f32[4,128]{1,0:T(4,128)S(1)} %pad_maximum_fusion.after_ref), channel_id=1, source_target_pairs={{64,0},{80,16},{96,32},{112,48},{0,64},{16,80},{32,96},{48,112},{1... | collective-permute-start | bytes 6152 | tf_op jit(solution)/shard_map/ppermute | solution.py:430
  15.7 2.9 %collective-permute-start.3 = (f32[4,128]{1,0:T(4,128)S(1)}, f32[4,128]{1,0:T(4,128)S(1)}, u32[]{:S(2)}, u32[]{:S(2)}) collective-permute-start(f32[4,128]{1,0:T(4,128)S(1)} %pad_maximum_fusion.after_ref), channel_id=1, source_target_pairs={{128,0},{144,16},{160,32},{176,48},{192,64},{208,80},{224,96},{240... | collective-permute-start | bytes 6152 | tf_op jit(solution)/shard_map/ppermute | solution.py:430
  18.6 0.2 collective-permute-start.4
  18.8 0.0 copy-done.10
  18.8 0.0 copy-start.7
  18.8 0.0 copy-start.8
  18.8 1.4 %shard_map.122 = (f32[16,128]{1,0:T(8,128)}, f32[16,128]{1,0:T(8,128)}) custom-call(f32[2,128,512]{2,1,0:T(8,128)} %grid_ref.1, f32[2,128,512]{2,1,0:T(8,128)} %grid_ref.1, f32[1,128]{1,0:T(1,128)} %bitcast.8, f32[4,128]{1,0:T(4,128)} %copy-done.10), custom_call_target="tpu_custom_call" | custom-call | flops 1000 | bytes 1000 | tf_op jit(solution)/shard_map/pallas_call | solution.py:439
  20.2 0.0 collective-permute-done.2
  20.2 0.5 collective-permute-done.3
  20.7 2.6 %collective-permute-done.4 = f32[4,128]{1,0:T(4,128)S(1)} collective-permute-done((f32[4,128]{1,0:T(4,128)S(1)}, f32[4,128]{1,0:T(4,128)S(1)}, u32[]{:S(2)}, u32[]{:S(2)}) %collective-permute-start.4) | collective-permute-done | bytes 2080 | tf_op jit(solution)/shard_map/ppermute | solution.py:430
  23.4 0.0 copy-start.5
  23.4 0.7 %concatenate.8.half_ref.after_ref = f32[32,128]{1,0:T(8,128)S(1)} concatenate(f32[2,128]{1,0:T(2,128)S(1)} %copy-done.11, f32[2,128]{1,0:T(2,128)S(1)} %collective-permute-done, f32[4,128]{1,0:T(4,128)S(1)} %collective-permute-done.2, f32[4,128]{1,0:T(4,128)S(1)} %collective-permute-done.3, f32[4,128]{1,0:T(4,128)S(1)} %collective-permute-done.4, f32[16,128]{1,0:T(8,128)} %get-tuple-element.11), dimensions={0} | concatenate | bytes 32768 | tf_op jit(solution)/shard_map/concatenate | solution.py:452
  24.1 0.0 copy-start.2
  24.1 0.0 copy-start.3
  24.1 0.0 copy-start.4
  24.1 0.0 collective-permute-start.5
  24.1 0.0 copy-done.5
  24.1 0.6 %copy-done.2 = f32[128]{0:T(128)S(1)} copy-done((f32[128]{0:T(128)S(1)}, f32[128]{0:T(128)}, u32[]{:S(2)}) %copy-start.2) | copy-done | bytes 536
  24.7 0.0 copy-done.3
  24.8 0.0 copy-done.4
  24.8 0.8 %shard_map.124 = (f32[16,1]{1,0:T(8,128)S(1)}, f32[16,1]{1,0:T(8,128)S(1)}) custom-call(f32[1,128]{1,0:T(1,128)S(1)} %bitcast.9, s32[1,128]{1,0:T(1,128)S(1)} %bitcast.11, f32[4]{0:T(128)S(1)} %copy-done.4, f32[4]{0:T(128)S(1)} %copy-done.5, f32[32,128]{1,0:T(8,128)S(1)} %concatenate.8.half_ref.after_ref), custom_call_target="tpu_custom_call" | custom-call | flops 1000 | bytes 1000 | tf_op jit(solution)/shard_map/pallas_call | solution.py:471
  25.6 0.0 copy-start.9
  25.6 1.6 %collective-permute-done.5.other_ref.far_ref = f32[32,128]{1,0:T(8,128)S(1)} collective-permute-done((f32[32,128]{1,0:T(8,128)S(1)}, f32[32,128]{1,0:T(8,128)S(1)}, u32[]{:S(2)}, u32[]{:S(2)}) %collective-permute-start.5) | collective-permute-done | bytes 16416 | tf_op jit(solution)/shard_map/ppermute | solution.py:453
  27.3 0.7 %shard_map.123.weight_ref = f32[528,128]{1,0:T(8,128)S(1)} custom-call(f32[32,128]{1,0:T(8,128)S(1)} %concatenate.8.half_ref.after_ref, f32[32,128]{1,0:T(8,128)S(1)} %collective-permute-done.5.other_ref.far_ref), custom_call_target="tpu_custom_call" | custom-call | flops 1000 | bytes 1000 | tf_op jit(solution)/shard_map/pallas_call | solution.py:457
  28.0 0.0 all-to-all-done.rows_ref
  28.0 0.0 copy-done.7
  28.0 0.0 copy-done.8
  28.0 0.0 copy-done.9
  28.0 2.6 %shard_map.125.after_ref = f32[1040,128]{1,0:T(8,128)} custom-call(f32[16,16,512]{2,1,0:T(8,128)S(1)} %all-to-all-done.rows_ref, f32[528,128]{1,0:T(8,128)S(1)} %shard_map.123.weight_ref, f32[16,1]{1,0:T(8,128)S(1)} %get-tuple-element.12.lattice_ref, f32[16,1]{1,0:T(8,128)S(1)} %get-tuple-element.13.gain_ref, bf16[2,256,256]{2,1,0:T(8,128)(2,1)S(1)} %copy-done.7, ...), custom_call_target="tpu_custom_call" | custom-call | flops 1000000000 | bytes 2097152 | tf_op jit(solution)/shard_map/pallas_call | solution.py:478
  30.6 0.0 copy-start.12
  30.6 0.0 copy-start
  30.6 0.0 copy-start.1
  30.6 6.5 %all-to-all-start.1 = ((f32[16,65,1,128]{3,2,1,0:T(1,128)}), f32[16,65,1,128]{3,2,1,0:T(1,128)S(1)}, u32[]{:S(2)}, u32[]{:S(2)}) async-start(f32[16,65,1,128]{3,2,1,0:T(1,128)} %bitcast.3), calls=%async_computation.1 | async-start | bytes 1064960 | tf_op jit(solution)/shard_map/all_to_all | solution.py:433
  37.1 0.0 copy-start.6
  37.1 0.0 copy-done.12
  37.1 0.1 collective-permute-start.1
  37.2 1.2 %collective-permute-done.1.near_ref = f32[16,128]{1,0:T(8,128)S(1)} collective-permute-done((f32[16,128]{1,0:T(8,128)S(1)}, f32[16,128]{1,0:T(8,128)S(1)}, u32[]{:S(2)}, u32[]{:S(2)}) %collective-permute-start.1) | collective-permute-done | bytes 8224 | tf_op jit(solution)/shard_map/ppermute | solution.py:430
  38.3 0.0 copy-done
  38.3 0.0 copy-done.1
  38.3 0.0 copy-done.6
  38.3 1.0 %shard_map.126 = (f32[2,128,512]{2,1,0:T(8,128)S(1)}, f32[1,128]{1,0:T(1,128)S(1)}) custom-call(f32[2,128,512]{2,1,0:T(8,128)S(1)} %copy-done, f32[16,128]{1,0:T(8,128)S(1)} %collective-permute-done.1.near_ref, f32[32,128]{1,0:T(8,128)S(1)} %collective-permute-done.5.other_ref.far_ref, f32[2,2,512]{2,1,0:T(2,128)S(1)} %copy-done.1, f32[1,128]{1,0:T(1,128)S(1)} %bitcast.10, ...), custom_call_target="tpu_custom_call" | custom-call | flops 1000 | bytes 1000 | tf_op jit(solution)/shard_map/pallas_call | solution.py:493
  39.3 11.5 %all-to-all-done.1 = f32[16,65,1,128]{3,2,1,0:T(1,128)S(1)} async-done(((f32[16,65,1,128]{3,2,1,0:T(1,128)}), f32[16,65,1,128]{3,2,1,0:T(1,128)S(1)}, u32[]{:S(2)}, u32[]{:S(2)}) %all-to-all-start.1) | async-done | bytes 532512 | tf_op jit(solution)/shard_map/all_to_all | solution.py:433
  50.9 0.9 %shard_map.127 = (f32[2,128,512]{2,1,0:T(8,128)}, f32[1,128]{1,0:T(1,128)}) custom-call(f32[2,128,512]{2,1,0:T(8,128)S(1)} %get-tuple-element.14.base_ref, f32[1040,128]{1,0:T(8,128)S(1)} %bitcast.7, f32[1,128]{1,0:T(1,128)S(1)} %get-tuple-element.15.still_ref), custom_call_target="tpu_custom_call" | custom-call | flops 1000000 | bytes 2097152 | tf_op jit(solution)/shard_map/pallas_call | solution.py:500
  (1 shorter events, 0.0 us)
Async XLA Ops:
  0.6 12.1 %copy-start.11 = (f32[2,128]{1,0:T(2,128)S(1)}, f32[2,128]{1,0:T(2,128)}, u32[]{:S(2)}) copy-start(f32[2,128]{1,0:T(2,128)} %param.12) | copy-start | bytes 3076
  0.6 27.3 %all-to-all-start = ((f32[16,16,512]{2,1,0:T(8,128)}), f32[16,16,512]{2,1,0:T(8,128)S(1)}, u32[]{:S(2)}, u32[]{:S(2)}) async-start(f32[16,16,512]{2,1,0:T(8,128)} %bitcast.6), calls=%async_computation | async-start | bytes 1048576 | tf_op jit(solution)/shard_map/all_to_all | solution.py:433
  12.7 1.2 %collective-permute-start = (f32[2,128]{1,0:T(2,128)S(1)}, f32[2,128]{1,0:T(2,128)S(1)}, u32[]{:S(2)}, u32[]{:S(2)}) collective-permute-start(f32[2,128]{1,0:T(2,128)S(1)} %copy-done.11), channel_id=1, source_target_pairs={{16,0},{0,16},{48,32},{32,48},{80,64},{64,80},{112,96},{96,112},{1... | collective-permute-start | bytes 3080 | tf_op jit(solution)/shard_map/ppermute | solution.py:430
  14.0 4.8 %copy-start.10 = (f32[4,128]{1,0:T(4,128)}, f32[4,128]{1,0:T(4,128)S(1)}, u32[]{:S(2)}) copy-start(f32[4,128]{1,0:T(4,128)S(1)} %pad_maximum_fusion.after_ref) | copy-start | bytes 6148
  14.0 6.2 %collective-permute-start.2 = (f32[4,128]{1,0:T(4,128)S(1)}, f32[4,128]{1,0:T(4,128)S(1)}, u32[]{:S(2)}, u32[]{:S(2)}) collective-permute-start(f32[4,128]{1,0:T(4,128)S(1)} %pad_maximum_fusion.after_ref), channel_id=1, source_target_pairs={{64,0},{80,16},{96,32},{112,48},{0,64},{16,80},{32,96},{48,112},{1... | collective-permute-start | bytes 6152 | tf_op jit(solution)/shard_map/ppermute | solution.py:430
  15.7 5.1 %collective-permute-start.3 = (f32[4,128]{1,0:T(4,128)S(1)}, f32[4,128]{1,0:T(4,128)S(1)}, u32[]{:S(2)}, u32[]{:S(2)}) collective-permute-start(f32[4,128]{1,0:T(4,128)S(1)} %pad_maximum_fusion.after_ref), channel_id=1, source_target_pairs={{128,0},{144,16},{160,32},{176,48},{192,64},{208,80},{224,96},{240... | collective-permute-start | bytes 6152 | tf_op jit(solution)/shard_map/ppermute | solution.py:430
  18.6 4.8 %collective-permute-start.4 = (f32[4,128]{1,0:T(4,128)S(1)}, f32[4,128]{1,0:T(4,128)S(1)}, u32[]{:S(2)}, u32[]{:S(2)}) collective-permute-start(f32[4,128]{1,0:T(4,128)S(1)} %pad_maximum_fusion.after_ref), channel_id=1, source_target_pairs={{192,0},{208,16},{224,32},{240,48},{128,64},{144,80},{160,96},{176... | collective-permute-start | bytes 6152 | tf_op jit(solution)/shard_map/ppermute | solution.py:430
  18.8 9.2 %copy-start.7 = (bf16[2,256,256]{2,1,0:T(8,128)(2,1)S(1)}, bf16[2,256,256]{2,1,0:T(8,128)(2,1)}, u32[]{:S(2)}) copy-start(bf16[2,256,256]{2,1,0:T(8,128)(2,1)} %constant.6.clone.ahead_ref) | copy-start | bytes 786436
  18.8 9.2 %copy-start.8 = (bf16[2,256,256]{2,1,0:T(8,128)(2,1)S(1)}, bf16[2,256,256]{2,1,0:T(8,128)(2,1)}, u32[]{:S(2)}) copy-start(bf16[2,256,256]{2,1,0:T(8,128)(2,1)} %constant.7.clone.back_ref) | copy-start | bytes 786436
  23.4 0.8 %copy-start.5 = (f32[4]{0:T(128)S(1)}, f32[4]{0:T(128)}, u32[]{:S(2)}) copy-start(f32[4]{0:T(128)} %populace_ref.3) | copy-start | bytes 52
  24.1 0.7 %copy-start.2 = (f32[128]{0:T(128)S(1)}, f32[128]{0:T(128)}, u32[]{:S(2)}) copy-start(f32[128]{0:T(128)} %param.14) | copy-start | bytes 1540
  24.1 0.7 %copy-start.3 = (s32[128]{0:T(128)S(1)}, s32[128]{0:T(128)}, u32[]{:S(2)}) copy-start(s32[128]{0:T(128)} %param.15) | copy-start | bytes 1540
  24.1 0.7 %copy-start.4 = (f32[4]{0:T(128)S(1)}, f32[4]{0:T(128)}, u32[]{:S(2)}) copy-start(f32[4]{0:T(128)} %damping_ref.3) | copy-start | bytes 52
  24.1 3.2 %collective-permute-start.5 = (f32[32,128]{1,0:T(8,128)S(1)}, f32[32,128]{1,0:T(8,128)S(1)}, u32[]{:S(2)}, u32[]{:S(2)}) collective-permute-start(f32[32,128]{1,0:T(8,128)S(1)} %concatenate.8.half_ref.after_ref), channel_id=1, source_target_pairs={{240,0},{32,16},{16,32},{64,48},{48,64},{96,80},{80,96},{128,112},... | collective-permute-start | bytes 49160 | tf_op jit(solution)/shard_map/ppermute | solution.py:453
  25.6 2.4 %copy-start.9 = (f32[33,2,128]{2,1,0:T(2,128)S(1)}, f32[33,2,128]{2,1,0:T(2,128)}, u32[]{:S(2)}) copy-start(f32[33,2,128]{2,1,0:T(2,128)} %constant.8.clone.twist_ref) | copy-start | bytes 101380
  30.6 6.5 %copy-start.12 = (f32[16,128]{1,0:T(8,128)S(1)}, f32[16,128]{1,0:T(8,128)}, u32[]{:S(2)}) copy-start(f32[16,128]{1,0:T(8,128)} %get-tuple-element.10) | copy-start | bytes 24580
  30.6 7.7 %copy-start = (f32[2,128,512]{2,1,0:T(8,128)S(1)}, f32[2,128,512]{2,1,0:T(8,128)}, u32[]{:S(2)}) copy-start(f32[2,128,512]{2,1,0:T(8,128)} %grid_ref.1) | copy-start | bytes 1572868
  30.6 7.7 %copy-start.1 = (f32[2,2,512]{2,1,0:T(2,128)S(1)}, f32[2,2,512]{2,1,0:T(2,128)}, u32[]{:S(2)}) copy-start(f32[2,2,512]{2,1,0:T(2,128)} %contact_ref.1) | copy-start | bytes 24580
  30.6 20.3 %all-to-all-start.1 = ((f32[16,65,1,128]{3,2,1,0:T(1,128)}), f32[16,65,1,128]{3,2,1,0:T(1,128)S(1)}, u32[]{:S(2)}, u32[]{:S(2)}) async-start(f32[16,65,1,128]{3,2,1,0:T(1,128)} %bitcast.3), calls=%async_computation.1 | async-start | bytes 1064960 | tf_op jit(solution)/shard_map/all_to_all | solution.py:433
  37.1 1.3 %copy-start.6 = (f32[4]{0:T(128)S(1)}, f32[4]{0:T(128)}, u32[]{:S(2)}) copy-start(f32[4]{0:T(128)} %conductance_ref.1) | copy-start | bytes 52
  37.1 1.3 %collective-permute-start.1 = (f32[16,128]{1,0:T(8,128)S(1)}, f32[16,128]{1,0:T(8,128)S(1)}, u32[]{:S(2)}, u32[]{:S(2)}) collective-permute-start(f32[16,128]{1,0:T(8,128)S(1)} %copy-done.12), channel_id=1, source_target_pairs={{16,0},{0,16},{48,32},{32,48},{80,64},{64,80},{112,96},{96,112},{1... | collective-permute-start | bytes 24584 | tf_op jit(solution)/shard_map/ppermute | solution.py:430
